TPU v7x, 32 devices: a whole 2x2x4 slice. The times are simulated.
32 devices in a mesh: seq: 4 (over y, x), tensor: 8 (over z, core).
Axes of the slice: x: 2, y: 2, z: 4, core: 2. Of those that a mesh axis runs over, the one named last changes fastest.
Arguments:
- hidden_in: bfloat16 [4096, 2304], P(('seq', 'tensor')), may hold values from -6 to 6
- norm_attn: float32 [2304], replicated, may hold values from 0.1 to 1.9
- norm_ffn: float32 [2304], replicated, may hold values from 0.1 to 1.9
- w_qkv: bfloat16 [3, 2304, 512], P(None, None, 'tensor'), may hold values from -1 to 1
- w_out: bfloat16 [512, 2304], P('tensor'), may hold values from -0.25 to 0.25
- w_router: float32 [2304, 8], replicated, may hold values from -4 to 4
- w_gate_up: bfloat16 [2, 23040, 2304], P(None, 'tensor'), may hold values from -0.125 to 0.125
- w_down: bfloat16 [23040, 2304], P('tensor'), may hold values from -0.109375 to 0.109375
- segment_ids: int32 [4096], P('seq'), may hold values from 0 to 7, never falling along the last dimension, each value on 1 to 3072 neighbouring positions
- expert_ids: int32 [4096, 2], P(('seq', 'tensor')), may hold values from 0 to 7, all different within a row; in each aligned block of 128 rows (0 to 127, 128 to 255, ...) at most 64 rows name the same one
Outputs:
- hidden_out: bfloat16 [4096, 2304], P(('seq', 'tensor'))
- kv_cache: bfloat16 [8, 4096, 128], P('tensor', 'seq')
Inputs may be any that keep to these rules, and one draw needn't show every extreme that they name: `segment_ids`: nondecreasing along the stream; each prompt has 1 to 3072 tokens and one has exactly 3072. `expert_ids`: the two experts of a token differ. Within each aligned block of 128 tokens (the tokens of one device), no expert is named by more than 64 tokens, a bound that some block reaches.
All inputs are finite; a program needn't handle non-finite values.
Results may differ from a plain program's by a relative error of at most 0.019.
Values may be sent and summed in bfloat16 or wider, within the bound.
A program may use at most 128 MiB of HBM per device.

v0:
```python
import math
import jax
import jax.numpy as jnp
from jax import lax
from jax.sharding import PartitionSpec as P

HD = 64
epsilon = 1e-06
low_score = -1e30


def rms_norm(hidden_rows, gain):
    as_float = hidden_rows.astype(jnp.float32)
    scale = lax.rsqrt(jnp.mean(as_float * as_float, axis=-1, keepdims=True) + epsilon)
    return (as_float * scale * gain).astype(jnp.bfloat16)


def rotate(head_rows, positions):
    half_size = head_rows.shape[-1] // 2
    frequency = jnp.exp(jnp.arange(half_size, dtype=jnp.float32) * (-math.log(10000.0) / half_size))
    angles = positions.astype(jnp.float32)[:, None] * frequency[None, :]
    cosine = jnp.cos(angles)[:, None, :]
    sine_part = jnp.sin(angles)[:, None, :]
    front_half = head_rows[..., :half_size]
    back_half = head_rows[..., half_size:]
    return jnp.concatenate(
        [front_half * cosine - back_half * sine_part, back_half * cosine + front_half * sine_part],
        axis=-1,
    )


def fold_keys(
    softmax_state, query_rows, query_segments, query_positions, kv_rows, key_segments, key_start
):
    running_max, denominator, weighted_sum = softmax_state
    row_count = kv_rows.shape[0]
    block_size = math.gcd(row_count, 2048)
    head_size = query_rows.shape[-1]
    for block_start in range(0, row_count, block_size):
        kv_block = kv_rows[block_start : block_start + block_size]
        key_block = kv_block[..., :head_size]
        value_block = kv_block[..., head_size:]
        segment_block = key_segments[block_start : block_start + block_size]
        position_block = key_start + block_start + jnp.arange(block_size, dtype=jnp.int32)
        scores = (
            jnp.einsum("qhd,khd->hqk", query_rows, key_block, preferred_element_type=jnp.float32)
            * 0.125
        )
        allowed = (query_segments[:, None] == segment_block[None, :]) & (
            position_block[None, :] <= query_positions[:, None]
        )
        masked = jnp.where(allowed[None], scores, low_score)
        new_max = jnp.maximum(running_max, jnp.max(masked, axis=-1))
        weights = jnp.where(allowed[None], jnp.exp(masked - new_max[..., None]), 0.0)
        factor = jnp.exp(running_max - new_max)
        denominator = denominator * factor + jnp.sum(weights, axis=-1)
        weighted_sum = weighted_sum * factor[:, None, :] + jnp.einsum(
            "hqk,khd->hdq",
            weights.astype(jnp.bfloat16),
            value_block,
            preferred_element_type=jnp.float32,
        )
        running_max = new_max
    return (running_max, denominator, weighted_sum)


def pack_ids(ids, width):
    flat = ids.reshape(-1).astype(jnp.bfloat16)
    row_count = -(-flat.shape[0] // (16 * width)) * 16
    return jnp.pad(flat, (0, row_count * width - flat.shape[0])).reshape(row_count, width)


def unpack_ids(packed, count):
    row_count = -(-count // packed.shape[-1])
    used = packed[..., :row_count, :]
    return used.reshape(packed.shape[:-2] + (-1,))[..., :count].astype(jnp.int32)


def slot_table(token_ids, target, slot_count):
    is_routed = jnp.any(token_ids == target, axis=1).astype(jnp.int32)
    places = jnp.arange(is_routed.shape[0], dtype=jnp.int32)
    slot_rank = (
        jnp.sum(jnp.where(places[None, :] <= places[:, None], is_routed[None, :], 0), axis=1) - 1
    )
    chosen_slot = (is_routed[None, :] == 1) & (
        slot_rank[None, :] == jnp.arange(slot_count, dtype=jnp.int32)[:, None]
    )
    return chosen_slot.astype(jnp.bfloat16)


def expert_apply(slot_rows, slot_ids, own_expert, w_router, w_gate_up, w_down):
    logits = jnp.dot(slot_rows.astype(jnp.float32), w_router, precision=lax.Precision.HIGHEST)
    expert_count = w_router.shape[1]
    one_hot = (
        slot_ids[:, :, None] == jnp.arange(expert_count, dtype=jnp.int32)[None, None, :]
    ).astype(jnp.float32)
    chosen = jnp.sum(one_hot * logits[:, None, :], axis=-1)
    gate_probs = jax.nn.softmax(chosen, axis=-1)
    weight = jnp.sum(jnp.where(slot_ids == own_expert, gate_probs, 0.0), axis=-1)
    contract = (((1,), (1,)), ((), ()))
    gate_act = lax.dot_general(
        slot_rows, w_gate_up[0], contract, preferred_element_type=jnp.float32
    )
    up_act = lax.dot_general(slot_rows, w_gate_up[1], contract, preferred_element_type=jnp.float32)
    hidden_act = (jax.nn.silu(gate_act) * up_act).astype(jnp.bfloat16)
    output = jnp.dot(hidden_act, w_down, preferred_element_type=jnp.float32)
    return (output * weight[:, None]).astype(jnp.bfloat16)


def shards(
    hidden_in,
    norm_attn,
    norm_ffn,
    w_qkv,
    w_out,
    w_router,
    w_gate_up,
    w_down,
    segment_ids,
    expert_ids,
):
    local_rows = hidden_in.shape[0]
    model_width = hidden_in.shape[1]
    tensor_count = lax.axis_size("tensor")
    tensor_place = lax.axis_index("tensor")
    seq_place = lax.axis_index("seq")
    group_rows = local_rows * tensor_count
    head_count = w_qkv.shape[2] // HD
    full_hidden = lax.all_gather(hidden_in, "tensor", axis=0, tiled=True)
    projected = jnp.einsum(
        "td,cdh->tch", rms_norm(full_hidden, norm_attn), w_qkv, preferred_element_type=jnp.float32
    )
    positions = seq_place * group_rows + jnp.arange(group_rows, dtype=jnp.int32)
    query_rows = rotate(projected[:, 0].reshape(group_rows, head_count, HD), positions).astype(
        jnp.bfloat16
    )
    key_rows = rotate(projected[:, 1].reshape(group_rows, head_count, HD), positions).astype(
        jnp.bfloat16
    )
    value_rows = projected[:, 2].reshape(group_rows, head_count, HD).astype(jnp.bfloat16)
    kv_rows = jnp.concatenate([key_rows, value_rows], axis=-1)
    kv_cache = kv_rows.transpose(1, 0, 2)
    seq_count = lax.axis_size("seq")
    kv_flat = kv_cache.reshape(head_count * group_rows, 2 * HD)
    kv_packed = jnp.concatenate([kv_flat, pack_ids(segment_ids, 2 * HD)], axis=0)
    out_packed = jnp.concatenate([w_out, pack_ids(expert_ids, model_width)], axis=0)
    kv_packed, out_packed = lax.optimization_barrier((kv_packed, out_packed))
    arrivals = []
    for step in range(1, seq_count):
        pairs = [(i, i ^ step) for i in range(seq_count)]
        arrivals.append((lax.ppermute(kv_packed, "seq", pairs), seq_place ^ step))
    out_gathered = lax.all_gather(out_packed, "tensor", axis=0)
    full_ids = unpack_ids(out_gathered[:, w_out.shape[0] :], 2 * local_rows)
    w_out_full = out_gathered[:, : w_out.shape[0]].reshape(-1, model_width)
    start_state = (
        jnp.full((head_count, group_rows), low_score, jnp.float32),
        jnp.zeros((head_count, group_rows), jnp.float32),
        jnp.zeros((head_count, HD, group_rows), jnp.float32),
    )
    softmax_state = fold_keys(
        start_state,
        query_rows,
        segment_ids,
        positions,
        kv_rows,
        segment_ids,
        seq_place * group_rows,
    )
    for arrived, source in arrivals:
        softmax_state = fold_keys(
            softmax_state,
            query_rows,
            segment_ids,
            positions,
            arrived[: kv_flat.shape[0]].reshape(head_count, group_rows, 2 * HD).transpose(1, 0, 2),
            unpack_ids(arrived[kv_flat.shape[0] :], group_rows),
            source * group_rows,
        )
    running_max, denominator, weighted_sum = softmax_state
    attended = (
        (weighted_sum / denominator[:, None, :])
        .astype(jnp.bfloat16)
        .reshape(head_count * HD, group_rows)
    )
    attended, w_out_full = lax.optimization_barrier((attended, w_out_full))
    attention_sum = lax.dot_general(
        lax.all_gather(attended, "tensor", axis=0, tiled=True),
        w_out_full,
        (((0,), (0,)), ((), ())),
        preferred_element_type=jnp.float32,
    )
    full_residual = full_hidden.astype(jnp.float32) + attention_sum
    full_rows = rms_norm(full_residual, norm_ffn)
    residual = lax.dynamic_slice_in_dim(full_residual, tensor_place * local_rows, local_rows, 0)
    expert_count = w_router.shape[1]
    slice_count = tensor_count // expert_count
    own_expert = tensor_place // slice_count
    slot_count = local_rows // 2
    block_ids = full_ids.reshape(tensor_count, local_rows, 2)
    slot_tables = jax.vmap(lambda source_ids: slot_table(source_ids, own_expert, slot_count))(
        block_ids
    )
    slot_rows = jnp.einsum(
        "sjr,srd->sjd",
        slot_tables,
        full_rows.reshape(tensor_count, local_rows, model_width),
        preferred_element_type=jnp.float32,
    ).astype(jnp.bfloat16)
    slot_ids = jnp.einsum(
        "sjr,srk->sjk", slot_tables.astype(jnp.float32), block_ids.astype(jnp.float32)
    ).astype(jnp.int32)
    term_rows = expert_apply(
        slot_rows.reshape(-1, model_width),
        slot_ids.reshape(-1, 2),
        own_expert,
        w_router,
        w_gate_up,
        w_down,
    )
    placed = jnp.einsum(
        "sjr,sjd->srd",
        slot_tables,
        term_rows.reshape(tensor_count, slot_count, model_width),
        preferred_element_type=jnp.float32,
    ).reshape(group_rows, model_width)
    expert_sum = lax.psum_scatter(
        placed.astype(jnp.bfloat16), "tensor", scatter_dimension=0, tiled=True
    ).astype(jnp.float32)
    hidden_out = (residual + expert_sum).astype(jnp.bfloat16)
    return (hidden_out, kv_cache)


def solution(mesh):
    placed = (
        P(("seq", "tensor"), None),
        P(),
        P(),
        P(None, None, "tensor"),
        P("tensor", None),
        P(),
        P(None, "tensor", None),
        P("tensor", None),
        P("seq"),
        P(("seq", "tensor"), None),
    )
    return jax.shard_map(
        shards,
        mesh=mesh,
        in_specs=placed,
        out_specs=(P(("seq", "tensor"), None), P("tensor", "seq", None)),
        check_vma=False,
    )
```

profile of v0, /device:TPU:0, one launch (start us, length us, event | category | flops | bytes accessed | tf_op | source)
XLA Modules:
  0.0 253.3 jit_solution(6927243527488938776)
XLA Ops:
  9.9 1.7 pad_maximum_fusion
  11.6 52.5 %all-gather.5.cloned.1.call-done = bf16[1024,2304]{1,0:T(8,128)(2,1)} async-done(((bf16[128,2304]{1,0:T(8,128)(2,1)}), bf16[1024,2304]{1,0:T(8,128)(2,1)}) %all-gather.5.cloned.1.call-update) | async-done | bytes 4718608 | tf_op jit(solution)/shard_map/all_gather | solution.py:129
  64.1 3.5 %fusion.6 = f32[1024]{0:T(1024)S(1)} fusion(bf16[1024,2304]{1,0:T(8,128)(2,1)} %all-gather.5.cloned.1.call-done), kind=kLoop, calls=%fused_computation.9 | loop fusion | flops 7076864 | bytes 4722688 | tf_op jit(solution)/shard_map/reduce_sum | solution.py:14
  67.9 1.8 fusion.11
  70.8 3.1 %fusion.76 = (bf16[1024,1,32]{2,0,1:T(8,128)(2,1)S(1)}, bf16[1024,1,32]{2,0,1:T(8,128)(2,1)S(1)}, bf16[1024,32]{1,0:T(8,128)(2,1)S(1)}, bf16[1024,32]{1,0:T(8,128)(2,1)}) fusion(f32[1024,1,32]{2,0,1:T(8,128)S(1)} %copy.84, f32[1024,1,32]{2,0,1:T(8,128)S(1)} %copy.83, f32[32]{0:T(128)S(1)} %multiply_exponential_fusion, f32[1024]{0:T(1024)S(1)} %fusion.107, ...), kind=kLoop, calls=%fused_computation.76 | loop fusion | flops 557056 | bytes 790656 | tf_op jit(solution)/shard_map/convert.9
  73.9 1.0 fusion.124
  74.9 1.5 collective-permute-start
  76.4 1.5 collective-permute-start.1
  78.8 1.1 pad_maximum_fusion.2
  80.7 3.5 %collective-permute-done = bf16[1040,128]{1,0:T(8,128)(2,1)S(1)} collective-permute-done((bf16[1040,128]{1,0:T(8,128)(2,1)S(1)}, bf16[1040,128]{1,0:T(8,128)(2,1)S(1)}, u32[]{:S(2)}, u32[]{:S(2)}) %collective-permute-start) | collective-permute-done | bytes 266272 | tf_op jit(solution)/shard_map/ppermute | solution.py:151
  84.9 5.5 %collective-permute-done.1 = bf16[1040,128]{1,0:T(8,128)(2,1)S(1)} collective-permute-done((bf16[1040,128]{1,0:T(8,128)(2,1)S(1)}, bf16[1040,128]{1,0:T(8,128)(2,1)S(1)}, u32[]{:S(2)}, u32[]{:S(2)}) %collective-permute-start.1) | collective-permute-done | bytes 266272 | tf_op jit(solution)/shard_map/ppermute | solution.py:151
  90.4 3.2 %fusion.18 = (f32[1024]{0:T(1024)S(1)}, f32[1024]{0:T(1024)S(1)}, f32[1024]{0:T(1024)S(1)}, f32[1024,1024]{0,1:T(8,128)S(1)}) fusion(s32[1024]{0:T(1024)S(1)} %get-tuple-element.56, s32[1024]{0:T(1024)S(1)} %copy-done.5, s32[1024]{0:T(1024)S(1)} %get-tuple-element.58, s32[1024]{0:T(1024)S(1)} %fusion.105, f32[1024,1024]{0,1:T(8,128)S(1)} %fusion.84, ...), kind=kOutput, calls=%fused_computation.36 | convolution fusion | flops 153089024 | bytes 13152256 | tf_op jit(solution)/shard_map/qhd,khd->hqk/dot_general | solution.py:46
  93.6 5.9 %fusion.20 = (f32[1024]{0:T(1024)S(1)}, f32[1024]{0:T(1024)S(1)}, f32[1024]{0:T(1024)S(1)}, f32[1024]{0:T(1024)S(1)}, f32[1024,1024]{0,1:T(8,128)S(1)}) fusion(f32[1024,1024]{0,1:T(8,128)S(1)} %fusion.84, f32[1024]{0:T(1024)S(1)} %get-tuple-element.46, s32[1024]{0:T(1024)S(1)} %get-tuple-element.56, s32[1024]{0:T(1024)S(1)} %copy-done.5, ...), kind=kOutput, calls=%fused_computation.38 | convolution fusion | flops 165670912 | bytes 17371136 | tf_op jit(solution)/shard_map/qhd,khd->hqk/dot_general | solution.py:46
  99.5 2.1 fusion.26
  101.7 1.8 fusion.32
  103.5 1.8 fusion.30
  105.3 1.4 fusion.54
  106.6 2.2 fusion.60
  108.9 5.2 %all-gather.9.cloned.1.call-done = bf16[640,2304]{1,0:T(8,128)(2,1)} async-done(((bf16[80,2304]{1,0:T(8,128)(2,1)}), bf16[640,2304]{1,0:T(8,128)(2,1)}) %all-gather.9.cloned.1.call-update) | async-done | bytes 2949136 | tf_op jit(solution)/shard_map/all_gather | solution.py:152
  114.1 1.8 slice.120
  116.2 1.0 slice.121
  118.5 18.6 %all-gather.7.cloned.1.call-done = bf16[512,1024]{1,0:T(8,128)(2,1)} async-done(((bf16[64,1024]{1,0:T(8,128)(2,1)}), bf16[512,1024]{1,0:T(8,128)(2,1)}) %all-gather.7.cloned.1.call-update) | async-done | bytes 1048592 | tf_op jit(solution)/shard_map/all_gather | solution.py:187
  137.1 6.1 %multiply_reduce_fusion = (f32[1024]{0:T(1024)S(1)}, f32[1024,2304]{1,0:T(8,128)S(1)}) fusion(bf16[512,1024]{1,0:T(8,128)(2,1)} %all-gather.7.cloned.1.call-done, bf16[512,2304]{1,0:T(8,128)(2,1)S(1)} %bitcast.110, bf16[1024,2304]{1,0:T(8,128)(2,1)} %all-gather.5.cloned.1.call-done), kind=kOutput, calls=%fused_computation.13 | convolution fusion | flops 2425355264 | bytes 17567744 | tf_op jit(solution)/shard_map/dot_general | solution.py:186
  143.2 0.9 multiply_convert_fusion
  144.1 2.7 %copy-done.2 = f32[1024,2304]{1,0:T(8,128)} copy-done((f32[1024,2304]{1,0:T(8,128)}, f32[1024,2304]{1,0:T(8,128)S(1)}, u32[]{:S(2)}) %copy-start.2) | copy-done | bytes 9437208
  146.8 0.8 convolution_convert_fusion.1
  147.7 1.9 fusion.129
  149.8 12.0 %fusion.2 = f32[512,2880]{0,1:T(8,128)} fusion(bf16[512,2304]{1,0:T(8,128)(2,1)S(1)} %bitcast.107, bf16[2,2880,2304]{2,1,0:T(8,128)(2,1)} %param.16), kind=kOutput, calls=%fused_computation.5 | convolution fusion | flops 6794772480 | bytes 21528576 | tf_op jit(solution)/shard_map/dot_general | solution.py:101
  162.0 22.0 %fusion.15 = bf16[512,2304]{1,0:T(8,128)(2,1)} fusion(bf16[2880,2304]{1,0:T(8,128)(2,1)} %param.17, f32[512]{0:T(512)S(1)} %mul.262, f32[512,2880]{0,1:T(8,128)} %fusion.2, bf16[512,2304]{1,0:T(8,128)(2,1)S(1)} %bitcast.108, bf16[2,2880,2304]{2,1,0:T(8,128)(2,1)} %param.16), kind=kOutput, calls=%fused_computation.21 | convolution fusion | flops 13600751616 | bytes 37160960 | tf_op jit(solution)/shard_map/dot_general | solution.py:106
  184.0 5.4 %convolution_convert_fusion = bf16[8,128,2304]{2,1,0:T(8,128)(2,1)} fusion(bf16[8,64,2304]{2,1,0:T(8,128)(2,1)} %bitcast.109, s32[8,128]{1,0:T(8,128)S(1)} %broadcast_add_fusion, pred[8,128]{1,0:T(8,128)(4,1)S(1)} %get-tuple-element.47), kind=kOutput, calls=%fused_computation.15 | convolution fusion | flops 304480256 | bytes 7083008 | tf_op jit(solution)/shard_map/sjr,sjd->srd/dot_general | solution.py:220
  189.4 54.7 %reduce-scatter.2.cloned.1.call-done = bf16[128,2304]{1,0:T(8,128)(2,1)} async-done(((bf16[1024,2304]{1,0:T(8,128)(2,1)}), bf16[128,2304]{1,0:T(8,128)(2,1)}) %reduce-scatter.2.cloned.1.call-update) | async-done | bytes 589840 | tf_op jit(solution)/shard_map/reduce_scatter | solution.py:226
  244.1 2.4 add_convert_fusion
  (81 shorter events, 8.4 us)
Async XLA Ops:
  7.2 60.4 %copy-start = (bf16[3,2304,64]{1,2,0:T(8,128)(2,1)S(1)}, bf16[3,2304,64]{1,2,0:T(8,128)(2,1)}, u32[]{:S(2)}) copy-start(bf16[3,2304,64]{1,2,0:T(8,128)(2,1)} %param.13) | copy-start | bytes 2654212
  7.2 60.4 %copy-start.7 = (f32[2304]{0:T(1024)S(1)}, f32[2304]{0:T(1024)}, u32[]{:S(2)}) copy-start(f32[2304]{0:T(1024)} %param.11) | copy-start | bytes 27652
  7.2 56.9 %all-gather.5.cloned.1.call-start = ((), (), s32[]{:S(2)}) async-start(), calls=%async_computation.1 | async-start | bytes 5308416 | tf_op jit(solution)/shard_map/all_gather | solution.py:129
  7.9 106.1 %all-gather.9.cloned.1.call-start = ((), (), s32[]{:S(2)}) async-start(), calls=%async_computation.4 | async-start | bytes 3317760 | tf_op jit(solution)/shard_map/all_gather | solution.py:152
  64.1 3.8 %copy-start.3 = (bf16[1024,2304]{1,0:T(8,128)(2,1)S(1)}, bf16[1024,2304]{1,0:T(8,128)(2,1)}, u32[]{:S(2)}) copy-start(bf16[1024,2304]{1,0:T(8,128)(2,1)} %all-gather.5.cloned.1.call-done) | copy-start | bytes 14155780
  74.9 9.3 %collective-permute-start = (bf16[1040,128]{1,0:T(8,128)(2,1)S(1)}, bf16[1040,128]{1,0:T(8,128)(2,1)S(1)}, u32[]{:S(2)}, u32[]{:S(2)}) collective-permute-start(bf16[1040,128]{1,0:T(8,128)(2,1)S(1)} %pad_maximum_fusion.1), channel_id=1, source_target_pairs={{0,8},{8,0},{16,24},{24,16},{1,9},{9,1},{17,25},{25,17},{2,10},{10... | collective-permute-start | bytes 798728 | tf_op jit(solution)/shard_map/ppermute | solution.py:151
  76.4 14.0 %collective-permute-start.1 = (bf16[1040,128]{1,0:T(8,128)(2,1)S(1)}, bf16[1040,128]{1,0:T(8,128)(2,1)S(1)}, u32[]{:S(2)}, u32[]{:S(2)}) collective-permute-start(bf16[1040,128]{1,0:T(8,128)(2,1)S(1)} %pad_maximum_fusion.1), channel_id=1, source_target_pairs={{0,16},{8,24},{16,0},{24,8},{1,17},{9,25},{17,1},{25,9},{2,18},{10... | collective-permute-start | bytes 798728 | tf_op jit(solution)/shard_map/ppermute | solution.py:151
  77.9 15.7 %collective-permute-start.2 = (bf16[1040,128]{1,0:T(8,128)(2,1)S(1)}, bf16[1040,128]{1,0:T(8,128)(2,1)S(1)}, u32[]{:S(2)}, u32[]{:S(2)}) collective-permute-start(bf16[1040,128]{1,0:T(8,128)(2,1)S(1)} %pad_maximum_fusion.1), channel_id=1, source_target_pairs={{0,24},{8,16},{16,8},{24,0},{1,25},{9,17},{17,9},{25,1},{2,26},{10... | collective-permute-start | bytes 798728 | tf_op jit(solution)/shard_map/ppermute | solution.py:151
  78.4 58.6 %all-gather.7.cloned.1.call-start = ((), (), s32[]{:S(2)}) async-start(), calls=%async_computation.2 | async-start | bytes 1179648 | tf_op jit(solution)/shard_map/all_gather | solution.py:187
  79.9 10.5 %copy-start.5 = (s32[1024]{0:T(1024)S(1)}, s32[1024]{0:T(1024)}, u32[]{:S(2)}) copy-start(s32[1024]{0:T(1024)} %param.18) | copy-start | bytes 12292
  115.9 128.2 %reduce-scatter.2.cloned.1.call-start = ((), (), s32[]{:S(2)}) async-start(), calls=%async_computation.3 | async-start | bytes 5308416 | tf_op jit(solution)/shard_map/reduce_scatter | solution.py:226
  118.5 24.7 %copy-start.6 = (f32[2304]{0:T(1024)S(1)}, f32[2304]{0:T(1024)}, u32[]{:S(2)}) copy-start(f32[2304]{0:T(1024)} %param.12) | copy-start | bytes 27652
  143.2 3.6 %copy-start.2 = (f32[1024,2304]{1,0:T(8,128)}, f32[1024,2304]{1,0:T(8,128)S(1)}, u32[]{:S(2)}) copy-start(f32[1024,2304]{1,0:T(8,128)S(1)} %get-tuple-element.52) | copy-start | bytes 28311556
  146.8 0.9 copy-start.4
  184.0 62.5 %copy-start.1 = (bf16[3,2304,64]{1,2,0:T(8,128)(2,1)S(1)}, bf16[3,2304,64]{1,2,0:T(8,128)(2,1)}, u32[]{:S(2)}) copy-start(bf16[3,2304,64]{1,2,0:T(8,128)(2,1)} %param.13) | copy-start | bytes 2654212
Sparse Core Ops, SparseCore 0:
  9.7 54.3 all-gather.4
  78.6 35.4 all-gather.8
  116.1 20.9 all-gather.6
  189.5 54.5 reduce-scatter.1
where the time goes:
time: 257 us; the launch traced here: 253 us
  waiting for transfers between devices  141 us (55%)
  matrix products  67.8 us (26%)
  other arithmetic  17.8 us (7%)
  between operations  14.4 us (6%)
  local copies, waits for them, and re-layouts  8.32 us (3%)
  starting transfers between devices  4.18 us (2%)
    reduce_scatter x1, waiting for transfers between devices, shards(): lax.psum_scatter(placed.astype(jnp.bfloat16), 'tensor', scatter_dimension...  54.7 us
    all_gather x1, waiting for transfers between devices, shards(): full_hidden = lax.all_gather(hidden_in, 'tensor', axis=0, tiled=True)  52.5 us
    dot_general x1, matrix products, expert_apply(): output = jnp.dot(hidden_act, w_down, preferred_element_type=jnp.float32)  22 us
    all_gather x1, waiting for transfers between devices, shards(): lax.all_gather(attended, 'tensor', axis=0, tiled=True)  18.6 us
    dot_general x1, matrix products, expert_apply(): lax.dot_general(slot_rows, w_gate_up[0], contract, preferred_element_type...  12 us
    dot_general x4, matrix products, fold_keys(): jnp.einsum('qhd,khd->hqk', query_rows, key_block, preferred_element_type=...  10.5 us
    ppermute x3, waiting for transfers between devices, shards(): arrivals.append((lax.ppermute(kv_packed, 'seq', pairs), seq_place ^ step))  8.96 us
    dot_general x4, matrix products, fold_keys(): jnp.einsum('hqk,khd->hdq', weights.astype(jnp.bfloat16), value_block, pre...  7.18 us
  transfers between devices with their start and end apart: 7, of which 6 were waited for; matrix products, arithmetic and copies ran while one was open for 11% of the time, Pallas kernels for 0%

commit v1 on v0

--- a/solution.py
+++ b/solution.py
@@ -3,6 +3,7 @@
 import jax.numpy as jnp
 from jax import lax
 from jax.sharding import PartitionSpec as P
+from jax.lax import axis_index, ppermute, psum
 
 HD = 64
 epsilon = 1e-06
@@ -126,7 +127,18 @@
     seq_place = lax.axis_index("seq")
     group_rows = local_rows * tensor_count
     head_count = w_qkv.shape[2] // HD
-    full_hidden = lax.all_gather(hidden_in, "tensor", axis=0, tiled=True)
+    num_devices = psum(1, "tensor")
+    shelf = []
+    for idx in tuple(range(num_devices)):
+        shelf.append((idx, (idx + 1) % num_devices))
+    a_next = [None] * num_devices
+    a_next[num_devices - 1] = hidden_in
+    for to_i in range(num_devices - 2, -1, -1):
+        a_next[to_i] = ppermute(a_next[to_i + 1], "tensor", shelf)
+    work_now = jnp.concatenate(a_next, axis=0)
+    built = axis_index("tensor")
+    b_next = (built + 1) * hidden_in.shape[0]
+    full_hidden = jnp.roll(work_now, b_next, axis=0)
     projected = jnp.einsum(
         "td,cdh->tch", rms_norm(full_hidden, norm_attn), w_qkv, preferred_element_type=jnp.float32
     )

time: 257 us -> 287 us (1.12)
  waiting for transfers between devices: 141 us -> 163 us
  local copies, waits for them, and re-layouts: 8.32 us -> 16.7 us
    ppermute x0 -> x7, waiting for transfers between devices: none -> 75.2 us  [shards(): a_next[to_i] = ppermute(a_next[to_i + 1], 'tensor', shelf)]
    all_gather x1 -> x0, waiting for transfers between devices: 52.5 us -> none  [shards(): full_hidden = lax.all_gather(hidden_in, 'tensor', axis=0, tiled=True)]
    unnamed x22 -> x47, local copies, waits for them, and re-layouts: 4.05 us -> 12.4 us
    ppermute x3, waiting for transfers between devices: 8.96 us -> 4.75 us  [shards(): arrivals.append((lax.ppermute(kv_packed, 'seq', pairs), seq_place ^ step))]
    all_gather x1, waiting for transfers between devices: 5.21 us -> 9.26 us  [shards(): out_gathered = lax.all_gather(out_packed, 'tensor', axis=0)]
  transfers between devices with their start and end apart: 7 -> 13, of which waited for: 6 -> 12; matrix products, arithmetic and copies ran while one was open for 11% -> 10% of each run, Pallas kernels for 0% -> 0%
where the time goes in v1:
time: 287 us; the launch traced here: 282 us
  waiting for transfers between devices  163 us (57%)
  matrix products  67.8 us (24%)
  local copies, waits for them, and re-layouts  16.7 us (6%)
  other arithmetic  15.3 us (5%)
  between operations  14.5 us (5%)
  starting transfers between devices  4.7 us (2%)
    ppermute x7, waiting for transfers between devices, shards(): a_next[to_i] = ppermute(a_next[to_i + 1], 'tensor', shelf)  75.2 us
    reduce_scatter x1, waiting for transfers between devices, shards(): lax.psum_scatter(placed.astype(jnp.bfloat16), 'tensor', scatter_dimension...  54.7 us
    dot_general x1, matrix products, expert_apply(): output = jnp.dot(hidden_act, w_down, preferred_element_type=jnp.float32)  22 us
    all_gather x1, waiting for transfers between devices, shards(): lax.all_gather(attended, 'tensor', axis=0, tiled=True)  18.7 us
    unnamed x47, local copies, waits for them, and re-layouts  12.4 us
    dot_general x1, matrix products, expert_apply(): lax.dot_general(slot_rows, w_gate_up[0], contract, preferred_element_type...  12 us
    dot_general x4, matrix products, fold_keys(): jnp.einsum('qhd,khd->hqk', query_rows, key_block, preferred_element_type=...  10.5 us
    all_gather x1, waiting for transfers between devices, shards(): out_gathered = lax.all_gather(out_packed, 'tensor', axis=0)  9.26 us
  transfers between devices with their start and end apart: 13, of which 12 were waited for; matrix products, arithmetic and copies ran while one was open for 10% of the time, Pallas kernels for 0%

profile of v1, /device:TPU:0, one launch (start us, length us, event | category | flops | bytes accessed | tf_op | source)
XLA Modules:
  0.0 281.9 jit_solution(2378951050063338345)
XLA Ops:
  7.7 11.8 %collective-permute-done = bf16[128,2304]{1,0:T(8,128)(2,1)S(1)} collective-permute-done((bf16[128,2304]{1,0:T(8,128)(2,1)}, bf16[128,2304]{1,0:T(8,128)(2,1)S(1)}, u32[]{:S(2)}, u32[]{:S(2)}) %collective-permute-start) | collective-permute-done | bytes 589856 | tf_op jit(solution)/shard_map/ppermute | solution.py:137
  19.6 11.1 %collective-permute-done.1 = bf16[128,2304]{1,0:T(8,128)(2,1)S(1)} collective-permute-done((bf16[128,2304]{1,0:T(8,128)(2,1)S(1)}, bf16[128,2304]{1,0:T(8,128)(2,1)S(1)}, u32[]{:S(2)}, u32[]{:S(2)}) %collective-permute-start.1) | collective-permute-done | bytes 589856 | tf_op jit(solution)/shard_map/ppermute | solution.py:137
  30.7 11.1 %collective-permute-done.2 = bf16[128,2304]{1,0:T(8,128)(2,1)S(1)} collective-permute-done((bf16[128,2304]{1,0:T(8,128)(2,1)S(1)}, bf16[128,2304]{1,0:T(8,128)(2,1)S(1)}, u32[]{:S(2)}, u32[]{:S(2)}) %collective-permute-start.2) | collective-permute-done | bytes 589856 | tf_op jit(solution)/shard_map/ppermute | solution.py:137
  41.8 11.1 %collective-permute-done.3 = bf16[128,2304]{1,0:T(8,128)(2,1)S(1)} collective-permute-done((bf16[128,2304]{1,0:T(8,128)(2,1)S(1)}, bf16[128,2304]{1,0:T(8,128)(2,1)S(1)}, u32[]{:S(2)}, u32[]{:S(2)}) %collective-permute-start.3) | collective-permute-done | bytes 589856 | tf_op jit(solution)/shard_map/ppermute | solution.py:137
  53.7 11.1 %collective-permute-done.4 = bf16[128,2304]{1,0:T(8,128)(2,1)S(1)} collective-permute-done((bf16[128,2304]{1,0:T(8,128)(2,1)S(1)}, bf16[128,2304]{1,0:T(8,128)(2,1)S(1)}, u32[]{:S(2)}, u32[]{:S(2)}) %collective-permute-start.4) | collective-permute-done | bytes 589856 | tf_op jit(solution)/shard_map/ppermute | solution.py:137
  65.5 10.5 %collective-permute-done.5 = bf16[128,2304]{1,0:T(8,128)(2,1)} collective-permute-done((bf16[128,2304]{1,0:T(8,128)(2,1)S(1)}, bf16[128,2304]{1,0:T(8,128)(2,1)}, u32[]{:S(2)}, u32[]{:S(2)}) %collective-permute-start.5) | collective-permute-done | bytes 589856 | tf_op jit(solution)/shard_map/ppermute | solution.py:137
  77.2 1.7 pad_maximum_fusion
  78.9 8.5 %collective-permute-done.6 = bf16[128,2304]{1,0:T(8,128)(2,1)} collective-permute-done((bf16[128,2304]{1,0:T(8,128)(2,1)}, bf16[128,2304]{1,0:T(8,128)(2,1)}, u32[]{:S(2)}, u32[]{:S(2)}) %collective-permute-start.6) | collective-permute-done | bytes 589856 | tf_op jit(solution)/shard_map/ppermute | solution.py:137
  90.8 1.2 constant_dynamic-update-slice_fusion.12
  95.7 1.8 fusion.11
  99.4 3.1 %fusion.77 = (bf16[1024,1,32]{2,0,1:T(8,128)(2,1)S(1)}, bf16[1024,1,32]{2,0,1:T(8,128)(2,1)S(1)}, bf16[1024,32]{1,0:T(8,128)(2,1)S(1)}, bf16[1024,32]{1,0:T(8,128)(2,1)}) fusion(f32[1024,1,32]{2,0,1:T(8,128)S(1)} %copy.84, f32[1024,1,32]{2,0,1:T(8,128)S(1)} %copy.83, f32[32]{0:T(128)S(1)} %multiply_exponential_fusion, f32[1024]{0:T(1024)S(1)} %fusion.108, ...), kind=kLoop, calls=%fused_computation.77 | loop fusion | flops 557056 | bytes 790656 | tf_op jit(solution)/shard_map/convert.9
  103.5 2.1 collective-permute-start.7
  105.5 1.5 collective-permute-start.8
  110.7 4.1 %collective-permute-done.8 = bf16[1040,128]{1,0:T(8,128)(2,1)S(1)} collective-permute-done((bf16[1040,128]{1,0:T(8,128)(2,1)S(1)}, bf16[1040,128]{1,0:T(8,128)(2,1)S(1)}, u32[]{:S(2)}, u32[]{:S(2)}) %collective-permute-start.8) | collective-permute-done | bytes 266272 | tf_op jit(solution)/shard_map/ppermute | solution.py:163
  114.8 3.2 %fusion.18 = (f32[1024]{0:T(1024)S(1)}, f32[1024]{0:T(1024)S(1)}, f32[1024]{0:T(1024)S(1)}, f32[1024,1024]{0,1:T(8,128)S(1)}) fusion(s32[1024]{0:T(1024)S(1)} %get-tuple-element.56, s32[1024]{0:T(1024)S(1)} %copy-done.10, s32[1024]{0:T(1024)S(1)} %get-tuple-element.58, s32[1024]{0:T(1024)S(1)} %fusion.106, f32[1024,1024]{0,1:T(8,128)S(1)} %fusion.85, ...), kind=kOutput, calls=%fused_computation.36 | convolution fusion | flops 153089024 | bytes 13152256 | tf_op jit(solution)/shard_map/qhd,khd->hqk/dot_general | solution.py:47
  118.1 5.9 %fusion.21 = (f32[1024]{0:T(1024)S(1)}, f32[1024]{0:T(1024)S(1)}, f32[1024]{0:T(1024)S(1)}, f32[1024]{0:T(1024)S(1)}, f32[1024,1024]{0,1:T(8,128)S(1)}) fusion(f32[1024,1024]{0,1:T(8,128)S(1)} %fusion.85, f32[1024]{0:T(1024)S(1)} %get-tuple-element.46, s32[1024]{0:T(1024)S(1)} %get-tuple-element.56, s32[1024]{0:T(1024)S(1)} %copy-done.10, ...), kind=kOutput, calls=%fused_computation.39 | convolution fusion | flops 165670912 | bytes 17371136 | tf_op jit(solution)/shard_map/qhd,khd->hqk/dot_general | solution.py:47
  124.0 2.1 fusion.27
  126.1 1.8 fusion.33
  127.9 1.8 fusion.31
  129.7 1.4 fusion.55
  131.1 2.2 fusion.61
  133.3 9.3 %all-gather.6.cloned.1.call-done = bf16[640,2304]{1,0:T(8,128)(2,1)} async-done(((bf16[80,2304]{1,0:T(8,128)(2,1)}), bf16[640,2304]{1,0:T(8,128)(2,1)}) %all-gather.6.cloned.1.call-update) | async-done | bytes 2949136 | tf_op jit(solution)/shard_map/all_gather | solution.py:164
  142.6 1.8 slice.120
  147.0 18.7 %all-gather.4.cloned.1.call-done = bf16[512,1024]{1,0:T(8,128)(2,1)} async-done(((bf16[64,1024]{1,0:T(8,128)(2,1)}), bf16[512,1024]{1,0:T(8,128)(2,1)}) %all-gather.4.cloned.1.call-update) | async-done | bytes 1048592 | tf_op jit(solution)/shard_map/all_gather | solution.py:199
  165.8 6.1 %multiply_reduce_fusion = (f32[1024]{0:T(1024)S(1)}, f32[1024,2304]{1,0:T(8,128)S(1)}) fusion(bf16[512,1024]{1,0:T(8,128)(2,1)} %all-gather.4.cloned.1.call-done, bf16[512,2304]{1,0:T(8,128)(2,1)S(1)} %bitcast.110, bf16[2048,2304]{1,0:T(8,128)(2,1)} %copy-done.3, s32[]{:T(128)S(6)} %select_n.61), kind=kOutput, calls=%fused_computation.13 | convolution fusion | flops 2425355264 | bytes 17567748 | tf_op jit(solution)/shard_map/dot_general | solution.py:198
  172.8 2.7 copy-done.2
  176.3 1.9 fusion.131
  178.5 12.0 %fusion.2 = f32[512,2880]{0,1:T(8,128)} fusion(bf16[512,2304]{1,0:T(8,128)(2,1)S(1)} %bitcast.107, bf16[2,2880,2304]{2,1,0:T(8,128)(2,1)} %param.16), kind=kOutput, calls=%fused_computation.5 | convolution fusion | flops 6794772480 | bytes 21528576 | tf_op jit(solution)/shard_map/dot_general | solution.py:102
  190.7 22.0 %fusion.15 = bf16[512,2304]{1,0:T(8,128)(2,1)} fusion(bf16[2880,2304]{1,0:T(8,128)(2,1)} %param.17, f32[512]{0:T(512)S(1)} %mul.266, f32[512,2880]{0,1:T(8,128)} %fusion.2, bf16[512,2304]{1,0:T(8,128)(2,1)S(1)} %bitcast.108, bf16[2,2880,2304]{2,1,0:T(8,128)(2,1)} %param.16), kind=kOutput, calls=%fused_computation.21 | convolution fusion | flops 13600751616 | bytes 37160960 | tf_op jit(solution)/shard_map/dot_general | solution.py:107
  212.6 5.4 %convolution_convert_fusion = bf16[8,128,2304]{2,1,0:T(8,128)(2,1)} fusion(bf16[8,64,2304]{2,1,0:T(8,128)(2,1)} %bitcast.109, s32[8,128]{1,0:T(8,128)S(1)} %broadcast_add_fusion, pred[8,128]{1,0:T(8,128)(4,1)S(1)} %get-tuple-element.47), kind=kOutput, calls=%fused_computation.15 | convolution fusion | flops 304480256 | bytes 7083008 | tf_op jit(solution)/shard_map/sjr,sjd->srd/dot_general | solution.py:232
  218.1 54.7 %reduce-scatter.2.cloned.1.call-done = bf16[128,2304]{1,0:T(8,128)(2,1)} async-done(((bf16[1024,2304]{1,0:T(8,128)(2,1)}), bf16[128,2304]{1,0:T(8,128)(2,1)}) %reduce-scatter.2.cloned.1.call-update) | async-done | bytes 589840 | tf_op jit(solution)/shard_map/reduce_scatter | solution.py:238
  272.8 2.4 add_convert_fusion
  (118 shorter events, 21.3 us)
Async XLA Ops:
  7.2 88.5 %copy-start = (bf16[3,2304,64]{1,2,0:T(8,128)(2,1)S(1)}, bf16[3,2304,64]{1,2,0:T(8,128)(2,1)}, u32[]{:S(2)}) copy-start(bf16[3,2304,64]{1,2,0:T(8,128)(2,1)} %param.13) | copy-start | bytes 2654212
  7.2 135.4 %all-gather.6.cloned.1.call-start = ((), (), s32[]{:S(2)}) async-start(), calls=%async_computation.3 | async-start | bytes 3317760 | tf_op jit(solution)/shard_map/all_gather | solution.py:164
  7.2 12.3 %collective-permute-start = (bf16[128,2304]{1,0:T(8,128)(2,1)}, bf16[128,2304]{1,0:T(8,128)(2,1)S(1)}, u32[]{:S(2)}, u32[]{:S(2)}) collective-permute-start(bf16[128,2304]{1,0:T(8,128)(2,1)} %param.10), channel_id=1, source_target_pairs={{0,1},{1,2},{2,3},{3,4},{4,5},{5,6},{6,7},{7,0},{8,9},{9,10},{10,1... | collective-permute-start | bytes 1769480 | tf_op jit(solution)/shard_map/ppermute | solution.py:137
  19.5 11.1 %collective-permute-start.1 = (bf16[128,2304]{1,0:T(8,128)(2,1)S(1)}, bf16[128,2304]{1,0:T(8,128)(2,1)S(1)}, u32[]{:S(2)}, u32[]{:S(2)}) collective-permute-start(bf16[128,2304]{1,0:T(8,128)(2,1)S(1)} %collective-permute-done), channel_id=1, source_target_pairs={{0,1},{1,2},{2,3},{3,4},{4,5},{5,6},{6,7},{7,0},{8,9},{9,10},{10,1... | collective-permute-start | bytes 1769480 | tf_op jit(solution)/shard_map/ppermute | solution.py:137
  30.7 11.1 %collective-permute-start.2 = (bf16[128,2304]{1,0:T(8,128)(2,1)S(1)}, bf16[128,2304]{1,0:T(8,128)(2,1)S(1)}, u32[]{:S(2)}, u32[]{:S(2)}) collective-permute-start(bf16[128,2304]{1,0:T(8,128)(2,1)S(1)} %collective-permute-done.1), channel_id=1, source_target_pairs={{0,1},{1,2},{2,3},{3,4},{4,5},{5,6},{6,7},{7,0},{8,9},{9,10},{10,1... | collective-permute-start | bytes 1769480 | tf_op jit(solution)/shard_map/ppermute | solution.py:137
  41.8 11.1 %collective-permute-start.3 = (bf16[128,2304]{1,0:T(8,128)(2,1)S(1)}, bf16[128,2304]{1,0:T(8,128)(2,1)S(1)}, u32[]{:S(2)}, u32[]{:S(2)}) collective-permute-start(bf16[128,2304]{1,0:T(8,128)(2,1)S(1)} %collective-permute-done.2), channel_id=1, source_target_pairs={{0,1},{1,2},{2,3},{3,4},{4,5},{5,6},{6,7},{7,0},{8,9},{9,10},{10,1... | collective-permute-start | bytes 1769480 | tf_op jit(solution)/shard_map/ppermute | solution.py:137
  52.9 0.8 copy-start.5
  53.7 11.1 %collective-permute-start.4 = (bf16[128,2304]{1,0:T(8,128)(2,1)S(1)}, bf16[128,2304]{1,0:T(8,128)(2,1)S(1)}, u32[]{:S(2)}, u32[]{:S(2)}) collective-permute-start(bf16[128,2304]{1,0:T(8,128)(2,1)S(1)} %collective-permute-done.3), channel_id=1, source_target_pairs={{0,1},{1,2},{2,3},{3,4},{4,5},{5,6},{6,7},{7,0},{8,9},{9,10},{10,1... | collective-permute-start | bytes 1769480 | tf_op jit(solution)/shard_map/ppermute | solution.py:137
  64.8 12.4 %copy-start.7 = (bf16[128,2304]{1,0:T(8,128)(2,1)}, bf16[128,2304]{1,0:T(8,128)(2,1)S(1)}, u32[]{:S(2)}) copy-start(bf16[128,2304]{1,0:T(8,128)(2,1)S(1)} %collective-permute-done.4) | copy-start | bytes 1769476
  64.8 11.2 %collective-permute-start.5 = (bf16[128,2304]{1,0:T(8,128)(2,1)S(1)}, bf16[128,2304]{1,0:T(8,128)(2,1)}, u32[]{:S(2)}, u32[]{:S(2)}) collective-permute-start(bf16[128,2304]{1,0:T(8,128)(2,1)S(1)} %collective-permute-done.4), channel_id=1, source_target_pairs={{0,1},{1,2},{2,3},{3,4},{4,5},{5,6},{6,7},{7,0},{8,9},{9,10},{10,1... | collective-permute-start | bytes 1769480 | tf_op jit(solution)/shard_map/ppermute | solution.py:137
  76.0 11.4 %collective-permute-start.6 = (bf16[128,2304]{1,0:T(8,128)(2,1)}, bf16[128,2304]{1,0:T(8,128)(2,1)}, u32[]{:S(2)}, u32[]{:S(2)}) collective-permute-start(bf16[128,2304]{1,0:T(8,128)(2,1)} %collective-permute-done.5), channel_id=1, source_target_pairs={{0,1},{1,2},{2,3},{3,4},{4,5},{5,6},{6,7},{7,0},{8,9},{9,10},{10,1... | collective-permute-start | bytes 1769480 | tf_op jit(solution)/shard_map/ppermute | solution.py:137
  78.9 13.2 %copy-start.4 = (bf16[128,2304]{1,0:T(8,128)(2,1)S(1)}, bf16[128,2304]{1,0:T(8,128)(2,1)}, u32[]{:S(2)}) copy-start(bf16[128,2304]{1,0:T(8,128)(2,1)} %param.10) | copy-start | bytes 1769476
  90.7 3.6 %copy-start.8 = (bf16[128,2304]{1,0:T(8,128)(2,1)S(1)}, bf16[128,2304]{1,0:T(8,128)(2,1)}, u32[]{:S(2)}) copy-start(bf16[128,2304]{1,0:T(8,128)(2,1)} %copy-done.7) | copy-start | bytes 1769476
  91.9 2.5 copy-start.6
  94.5 1.2 copy-start.12
  94.7 3.6 %copy-start.3 = (bf16[2048,2304]{1,0:T(8,128)(2,1)}, bf16[2048,2304]{1,0:T(8,128)(2,1)S(1)}, u32[]{:S(2)}) copy-start(bf16[2048,2304]{1,0:T(8,128)(2,1)S(1)} %constant_dynamic-update-slice_fusion) | copy-start | bytes 28311556
  103.5 6.5 %collective-permute-start.7 = (bf16[1040,128]{1,0:T(8,128)(2,1)S(1)}, bf16[1040,128]{1,0:T(8,128)(2,1)S(1)}, u32[]{:S(2)}, u32[]{:S(2)}) collective-permute-start(bf16[1040,128]{1,0:T(8,128)(2,1)S(1)} %pad_maximum_fusion.1), channel_id=1, source_target_pairs={{0,8},{8,0},{16,24},{24,16},{1,9},{9,1},{17,25},{25,17},{2,10},{10... | collective-permute-start | bytes 798728 | tf_op jit(solution)/shard_map/ppermute | solution.py:163
  105.5 9.3 %collective-permute-start.8 = (bf16[1040,128]{1,0:T(8,128)(2,1)S(1)}, bf16[1040,128]{1,0:T(8,128)(2,1)S(1)}, u32[]{:S(2)}, u32[]{:S(2)}) collective-permute-start(bf16[1040,128]{1,0:T(8,128)(2,1)S(1)} %pad_maximum_fusion.1), channel_id=1, source_target_pairs={{0,16},{8,24},{16,0},{24,8},{1,17},{9,25},{17,1},{25,9},{2,18},{10... | collective-permute-start | bytes 798728 | tf_op jit(solution)/shard_map/ppermute | solution.py:163
  107.0 11.0 %collective-permute-start.9 = (bf16[1040,128]{1,0:T(8,128)(2,1)S(1)}, bf16[1040,128]{1,0:T(8,128)(2,1)S(1)}, u32[]{:S(2)}, u32[]{:S(2)}) collective-permute-start(bf16[1040,128]{1,0:T(8,128)(2,1)S(1)} %pad_maximum_fusion.1), channel_id=1, source_target_pairs={{0,24},{8,16},{16,8},{24,0},{1,25},{9,17},{17,9},{25,1},{2,26},{10... | collective-permute-start | bytes 798728 | tf_op jit(solution)/shard_map/ppermute | solution.py:163
  107.1 58.7 %all-gather.4.cloned.1.call-start = ((), (), s32[]{:S(2)}) async-start(), calls=%async_computation.1 | async-start | bytes 1179648 | tf_op jit(solution)/shard_map/all_gather | solution.py:199
  108.5 6.3 %copy-start.10 = (s32[1024]{0:T(1024)S(1)}, s32[1024]{0:T(1024)}, u32[]{:S(2)}) copy-start(s32[1024]{0:T(1024)} %param.18) | copy-start | bytes 12292
  144.5 128.3 %reduce-scatter.2.cloned.1.call-start = ((), (), s32[]{:S(2)}) async-start(), calls=%async_computation.2 | async-start | bytes 5308416 | tf_op jit(solution)/shard_map/reduce_scatter | solution.py:238
  147.0 24.8 %copy-start.11 = (f32[2304]{0:T(1024)S(1)}, f32[2304]{0:T(1024)}, u32[]{:S(2)}) copy-start(f32[2304]{0:T(1024)} %param.12) | copy-start | bytes 27652
  171.8 3.6 %copy-start.2 = (f32[1024,2304]{1,0:T(8,128)}, f32[1024,2304]{1,0:T(8,128)S(1)}, u32[]{:S(2)}) copy-start(f32[1024,2304]{1,0:T(8,128)S(1)} %get-tuple-element.52) | copy-start | bytes 28311556
  175.5 0.9 copy-start.9
  212.6 62.5 %copy-start.1 = (bf16[3,2304,64]{1,2,0:T(8,128)(2,1)S(1)}, bf16[3,2304,64]{1,2,0:T(8,128)(2,1)}, u32[]{:S(2)}) copy-start(bf16[3,2304,64]{1,2,0:T(8,128)(2,1)} %param.13) | copy-start | bytes 2654212
Sparse Core Ops, SparseCore 0:
  107.2 35.3 all-gather.5
  144.8 20.9 all-gather.3
  218.2 54.5 reduce-scatter.1
